TPU v7x, 32 devices: a whole 2x2x4 slice. The times are simulated.
32 devices in a mesh: space: 16 (over z, y, core), chan: 2 (over x).
Axes of the slice: x: 2, y: 2, z: 4, core: 2. Of those that a mesh axis runs over, the one named last changes fastest.
Arguments:
- field_in: bfloat16 [128, 512, 128], P('space', 'chan'), may hold values from -6 to 6
- kernel_first: bfloat16 [3, 3, 3, 512, 512], P(None, None, None, 'chan'), may hold values from -0.0546875 to 0.0546875
- bias_first: float32 [512], P('chan'), may hold values from -3 to 3
- kernel_second: bfloat16 [3, 3, 3, 512, 512], P(None, None, None, 'chan'), may hold values from -0.0546875 to 0.0546875
- bias_second: float32 [512], P('chan'), may hold values from -3 to 3
Outputs:
- field_out: bfloat16 [128, 512, 128], P('space', 'chan')
All inputs are finite; a program needn't handle non-finite values.
Results may differ from a plain program's by a relative error of at most 0.0048.
Values may be sent and summed in bfloat16 or wider, within the bound.
A program may use at most 64 MiB of HBM per device.

v0:
```python
import jax
import jax.numpy as jnp
from jax import lax
from jax.sharding import PartitionSpec as P

DILATION = 4
NY = 8
NX = 16


def with_halo(value, sides, width):
    for axis, dim in sides:
        size, length = (lax.axis_size(axis), value.shape[dim])
        up = [(i, (i + 1) % size) for i in range(size - 1)]
        down = [(j, i) for i, j in up]
        last = lax.slice_in_dim(value, length - width, length, axis=dim)
        leading = lax.slice_in_dim(value, 0, width, axis=dim)
        before = lax.ppermute(last, axis, up)
        after = lax.ppermute(leading, axis, down)
        value = jnp.concatenate([before, value, after], axis=dim)
    return value


def apply_taps(slab_in, taps_in):
    layers = slab_in.shape[0] - 2 * DILATION
    places = lax.iota(jnp.int32, NY * NX)
    row_of = places // NX
    col_of = places % NX
    summed = jnp.zeros((layers, taps_in.shape[3], NY * NX), jnp.float32)
    for second in range(3):
        for third in range(3):
            step_y = DILATION * (second - 1)
            step_x = DILATION * (third - 1)
            offset = step_y * NX + step_x
            moved = jnp.roll(slab_in, -offset, axis=2) if offset != 0 else slab_in
            inside = (
                (row_of + step_y >= 0)
                & (row_of + step_y < NY)
                & (col_of + step_x >= 0)
                & (col_of + step_x < NX)
            ).astype(jnp.float32)
            partial_value = jnp.zeros_like(summed)
            for first in range(3):
                window = moved[first * DILATION : first * DILATION + layers]
                partial_value = partial_value + jnp.einsum(
                    "oi,zip->zop",
                    taps_in[first, second, third],
                    window,
                    preferred_element_type=jnp.float32,
                )
            summed = summed + partial_value * inside[None, None, :]
    return summed


def conv_block(local_field, kernel, bias):
    whole = lax.all_gather(local_field, "chan", axis=1, tiled=True)
    bordered = with_halo(whole, (("space", 0),), DILATION)
    pre = apply_taps(bordered, kernel)
    active = jax.nn.gelu(pre + bias[None, :, None], approximate=True)
    return (local_field.astype(jnp.float32) + active).astype(jnp.bfloat16)


def per_device(field_in, kernel_first, bias_first, kernel_second, bias_second):
    middle = conv_block(field_in, kernel_first, bias_first)
    return conv_block(middle, kernel_second, bias_second)


def solution(mesh):
    placed = (
        P("space", "chan", None),
        P(None, None, None, "chan", None),
        P("chan"),
        P(None, None, None, "chan", None),
        P("chan"),
    )
    return jax.shard_map(
        per_device, mesh=mesh, in_specs=placed, out_specs=P("space", "chan", None), check_vma=False
    )
```

profile of v0, /device:TPU:1, one launch (start us, length us, event | category | flops | bytes accessed | tf_op | source)
XLA Modules:
  0.0 131.4 jit_solution(11794609462427958268)
XLA Ops:
  6.5 2.0 %copy.6 = bf16[8,256,128]{1,2,0:T(8,128)(2,1)} copy(bf16[8,256,128]{2,1,0:T(8,128)(2,1)} %param.5) | data formatting | bytes 1048576 | tf_op args[0]
  8.7 23.5 %all-gather.3.cloned.1.call-done = bf16[8,512,128]{1,2,0:T(8,128)(2,1)} async-done(((bf16[8,256,128]{1,2,0:T(8,128)(2,1)}), bf16[8,512,128]{1,2,0:T(8,128)(2,1)}) %all-gather.3.cloned.1.call-update) | async-done | bytes 1048592 | tf_op jit(solution)/shard_map/all_gather | solution.py:56
  32.3 1.4 %fusion.309 = (bf16[4,512,128]{1,2,0:T(8,128)(2,1)S(1)}, bf16[4,512,128]{1,2,0:T(8,128)(2,1)S(1)}) fusion(bf16[8,512,128]{1,2,0:T(8,128)(2,1)} %all-gather.3.cloned.1.call-done), kind=kLoop, calls=%fused_computation.317 | loop fusion | bytes 2097152 | tf_op jit(solution)/shard_map/slice | solution.py:17
  33.6 3.7 %collective-permute-start = (bf16[4,512,128]{1,2,0:T(8,128)(2,1)S(1)}, bf16[4,512,128]{1,2,0:T(8,128)(2,1)S(1)}, u32[]{:S(2)}, u32[]{:S(2)}) collective-permute-start(bf16[4,512,128]{1,2,0:T(8,128)(2,1)S(1)} %get-tuple-element.28), channel_id=1, source_target_pairs={{0,2},{2,4},{4,6},{6,8},{8,10},{10,12},{12,14},{14,16},{16,18},{18... | collective-permute-start | bytes 1572872 | tf_op jit(solution)/shard_map/ppermute | solution.py:18
  37.3 1.9 %collective-permute-start.1 = (bf16[4,512,128]{1,2,0:T(8,128)(2,1)S(1)}, bf16[4,512,128]{1,2,0:T(8,128)(2,1)S(1)}, u32[]{:S(2)}, u32[]{:S(2)}) collective-permute-start(bf16[4,512,128]{1,2,0:T(8,128)(2,1)S(1)} %get-tuple-element.27), channel_id=1, source_target_pairs={{2,0},{4,2},{6,4},{8,6},{10,8},{12,10},{14,12},{16,14},{18,16},{20... | collective-permute-start | bytes 1572872 | tf_op jit(solution)/shard_map/ppermute | solution.py:19
  39.3 1.4 %fusion.207 = f32[8,128,256]{2,1,0:T(8,128)S(1)} fusion(bf16[8,512,128]{1,2,0:T(8,128)(2,1)S(1)} %copy-done, bf16[3,3,3,256,512]{4,3,2,1,0:T(8,128)(2,1)} %param.6), kind=kOutput, calls=%fused_computation.186 | convolution fusion | flops 268435456 | bytes 2359296 | tf_op jit(solution)/shard_map/oi,zip->zop/dot_general | solution.py:45
  40.7 8.3 %collective-permute-done = bf16[4,512,128]{1,2,0:T(8,128)(2,1)S(1)} collective-permute-done((bf16[4,512,128]{1,2,0:T(8,128)(2,1)S(1)}, bf16[4,512,128]{1,2,0:T(8,128)(2,1)S(1)}, u32[]{:S(2)}, u32[]{:S(2)}) %collective-permute-start) | collective-permute-done | bytes 524320 | tf_op jit(solution)/shard_map/ppermute | solution.py:18
  49.2 0.5 fusion.305
  50.2 1.0 slice-done
  51.2 0.9 slice-done.1
  55.3 1.2 fusion.304
  57.4 0.5 fusion.144
  57.9 0.5 fusion.145
  58.4 0.5 fusion.213
  58.9 0.5 fusion.215
  60.3 0.5 fusion.223
  61.3 0.5 fusion.76
  61.7 0.5 fusion.74
  62.2 0.5 fusion.72
  62.7 0.5 fusion.70
  63.2 0.5 fusion.68
  63.8 0.5 fusion.66
  64.7 0.6 fusion.62
  65.9 0.5 copy-done.2
  66.4 1.9 %fusion.126 = bf16[8,256,128]{1,2,0:T(8,128)(2,1)} fusion(f32[8,128,256]{2,1,0:T(8,128)S(1)} %fusion.76, f32[8,128,256]{2,1,0:T(8,128)S(1)} %fusion.74, f32[8,128,256]{2,1,0:T(8,128)S(1)} %fusion.72, f32[8,128,256]{2,1,0:T(8,128)S(1)} %fusion.70, f32[8,128,256]{2,1,0:T(8,128)S(1)} %fusion.62, f32[8,128,256]{2,1,0:T(8,128)S(1)} %fusion.4, ...), kind=kOutput, calls=%fused_computation.110 | convolution fusion | flops 276824064 | bytes 10225152 | tf_op jit(solution)/shard_map/oi,zip->zop/dot_general | solution.py:45
  68.3 21.3 %all-gather.5.cloned.1.call-done = bf16[8,512,128]{1,2,0:T(8,128)(2,1)} async-done(((bf16[8,256,128]{1,2,0:T(8,128)(2,1)}), bf16[8,512,128]{1,2,0:T(8,128)(2,1)}) %all-gather.5.cloned.1.call-update) | async-done | bytes 1048592 | tf_op jit(solution)/shard_map/all_gather | solution.py:56
  89.6 1.4 %fusion.308 = (bf16[4,512,128]{1,2,0:T(8,128)(2,1)S(1)}, bf16[4,512,128]{1,2,0:T(8,128)(2,1)S(1)}) fusion(bf16[8,512,128]{1,2,0:T(8,128)(2,1)} %all-gather.5.cloned.1.call-done), kind=kLoop, calls=%fused_computation.316 | loop fusion | bytes 2097152 | tf_op jit(solution)/shard_map/slice | solution.py:17
  90.9 3.7 %collective-permute-start.2 = (bf16[4,512,128]{1,2,0:T(8,128)(2,1)S(1)}, bf16[4,512,128]{1,2,0:T(8,128)(2,1)S(1)}, u32[]{:S(2)}, u32[]{:S(2)}) collective-permute-start(bf16[4,512,128]{1,2,0:T(8,128)(2,1)S(1)} %get-tuple-element.26), channel_id=1, source_target_pairs={{0,2},{2,4},{4,6},{6,8},{8,10},{10,12},{12,14},{14,16},{16,18},{18... | collective-permute-start | bytes 1572872 | tf_op jit(solution)/shard_map/ppermute | solution.py:18
  94.6 2.1 %collective-permute-start.3 = (bf16[4,512,128]{1,2,0:T(8,128)(2,1)S(1)}, bf16[4,512,128]{1,2,0:T(8,128)(2,1)S(1)}, u32[]{:S(2)}, u32[]{:S(2)}) collective-permute-start(bf16[4,512,128]{1,2,0:T(8,128)(2,1)S(1)} %get-tuple-element.25), channel_id=1, source_target_pairs={{2,0},{4,2},{6,4},{8,6},{10,8},{12,10},{14,12},{16,14},{18,16},{20... | collective-permute-start | bytes 1572872 | tf_op jit(solution)/shard_map/ppermute | solution.py:19
  96.7 1.6 %fusion.167 = f32[8,128,256]{2,1,0:T(8,128)S(1)} fusion(bf16[8,512,128]{1,2,0:T(8,128)(2,1)S(1)} %copy-done.1, bf16[3,3,3,256,512]{4,3,2,1,0:T(8,128)(2,1)} %param.8), kind=kOutput, calls=%fused_computation.146 | convolution fusion | flops 268435456 | bytes 2359296 | tf_op jit(solution)/shard_map/oi,zip->zop/dot_general | solution.py:45
  98.3 8.0 %collective-permute-done.2 = bf16[4,512,128]{1,2,0:T(8,128)(2,1)S(1)} collective-permute-done((bf16[4,512,128]{1,2,0:T(8,128)(2,1)S(1)}, bf16[4,512,128]{1,2,0:T(8,128)(2,1)S(1)}, u32[]{:S(2)}, u32[]{:S(2)}) %collective-permute-start.2) | collective-permute-done | bytes 524320 | tf_op jit(solution)/shard_map/ppermute | solution.py:18
  106.5 0.5 fusion.300
  107.5 0.8 slice-done.3
  110.9 0.5 fusion.160
  111.5 1.2 fusion.299
  113.6 0.5 fusion.140
  114.1 0.5 fusion.141
  115.0 0.5 fusion.175
  117.4 0.5 fusion.95
  117.9 0.5 fusion.93
  118.4 0.5 fusion.91
  118.8 0.5 fusion.89
  119.3 0.5 fusion.87
  119.9 0.5 fusion.85
  120.8 0.6 fusion.81
  121.9 0.5 copy-done.3
  122.5 1.0 add_convert_fusion
  123.5 1.0 copy.8
  (71 shorter events, 14.5 us)
Async XLA Ops:
  6.5 25.7 %all-gather.3.cloned.1.call-start = ((), (), s32[]{:S(2)}) async-start(), calls=%async_computation | async-start | bytes 1572864 | tf_op jit(solution)/shard_map/all_gather | solution.py:56
  8.6 81.0 %all-gather.5.cloned.1.call-start = ((), (), s32[]{:S(2)}) async-start(), calls=%async_computation.1 | async-start | bytes 1572864 | tf_op jit(solution)/shard_map/all_gather | solution.py:56
  32.3 7.0 %copy-start = (bf16[8,512,128]{1,2,0:T(8,128)(2,1)S(1)}, bf16[8,512,128]{1,2,0:T(8,128)(2,1)}, u32[]{:S(2)}) copy-start(bf16[8,512,128]{1,2,0:T(8,128)(2,1)} %all-gather.3.cloned.1.call-done) | copy-start | bytes 3145732
  33.6 15.4 %collective-permute-start = (bf16[4,512,128]{1,2,0:T(8,128)(2,1)S(1)}, bf16[4,512,128]{1,2,0:T(8,128)(2,1)S(1)}, u32[]{:S(2)}, u32[]{:S(2)}) collective-permute-start(bf16[4,512,128]{1,2,0:T(8,128)(2,1)S(1)} %get-tuple-element.28), channel_id=1, source_target_pairs={{0,2},{2,4},{4,6},{6,8},{8,10},{10,12},{12,14},{14,16},{16,18},{18... | collective-permute-start | bytes 1572872 | tf_op jit(solution)/shard_map/ppermute | solution.py:18
  37.3 11.8 %collective-permute-start.1 = (bf16[4,512,128]{1,2,0:T(8,128)(2,1)S(1)}, bf16[4,512,128]{1,2,0:T(8,128)(2,1)S(1)}, u32[]{:S(2)}, u32[]{:S(2)}) collective-permute-start(bf16[4,512,128]{1,2,0:T(8,128)(2,1)S(1)} %get-tuple-element.27), channel_id=1, source_target_pairs={{2,0},{4,2},{6,4},{8,6},{10,8},{12,10},{14,12},{16,14},{18,16},{20... | collective-permute-start | bytes 1572872 | tf_op jit(solution)/shard_map/ppermute | solution.py:19
  49.0 2.2 %slice-start = ((s8[7077888]{0:T(1024)(128)(4,1)}), s8[4194304]{0:T(1024)(128)(4,1)S(1)}, s32[]{:S(2)}) async-start(s8[7077888]{0:T(1024)(128)(4,1)} %bitcast.286), calls=%async_computation.2 | async-start | bytes 8388608
  49.2 3.0 %slice-start.1 = ((s8[7077888]{0:T(1024)(128)(4,1)}), s8[2883584]{0:T(1024)(128)(4,1)S(1)}, s32[]{:S(2)}) async-start(s8[7077888]{0:T(1024)(128)(4,1)} %bitcast.286), calls=%async_computation.3 | async-start | bytes 5767168
  65.4 1.0 copy-start.2
  65.4 1.0 copy-start.4
  89.6 7.1 %copy-start.1 = (bf16[8,512,128]{1,2,0:T(8,128)(2,1)S(1)}, bf16[8,512,128]{1,2,0:T(8,128)(2,1)}, u32[]{:S(2)}) copy-start(bf16[8,512,128]{1,2,0:T(8,128)(2,1)} %all-gather.5.cloned.1.call-done) | copy-start | bytes 3145732
  90.9 15.4 %collective-permute-start.2 = (bf16[4,512,128]{1,2,0:T(8,128)(2,1)S(1)}, bf16[4,512,128]{1,2,0:T(8,128)(2,1)S(1)}, u32[]{:S(2)}, u32[]{:S(2)}) collective-permute-start(bf16[4,512,128]{1,2,0:T(8,128)(2,1)S(1)} %get-tuple-element.26), channel_id=1, source_target_pairs={{0,2},{2,4},{4,6},{6,8},{8,10},{10,12},{12,14},{14,16},{16,18},{18... | collective-permute-start | bytes 1572872 | tf_op jit(solution)/shard_map/ppermute | solution.py:18
  94.6 11.8 %collective-permute-start.3 = (bf16[4,512,128]{1,2,0:T(8,128)(2,1)S(1)}, bf16[4,512,128]{1,2,0:T(8,128)(2,1)S(1)}, u32[]{:S(2)}, u32[]{:S(2)}) collective-permute-start(bf16[4,512,128]{1,2,0:T(8,128)(2,1)S(1)} %get-tuple-element.25), channel_id=1, source_target_pairs={{2,0},{4,2},{6,4},{8,6},{10,8},{12,10},{14,12},{16,14},{18,16},{20... | collective-permute-start | bytes 1572872 | tf_op jit(solution)/shard_map/ppermute | solution.py:19
  96.7 10.8 %slice-start.2 = ((s8[7077888]{0:T(1024)(128)(4,1)}), s8[4194304]{0:T(1024)(128)(4,1)S(1)}, s32[]{:S(2)}) async-start(s8[7077888]{0:T(1024)(128)(4,1)} %bitcast.288), calls=%async_computation.4 | async-start | bytes 8388608
  106.5 1.8 %slice-start.3 = ((s8[7077888]{0:T(1024)(128)(4,1)}), s8[2883584]{0:T(1024)(128)(4,1)S(1)}, s32[]{:S(2)}) async-start(s8[7077888]{0:T(1024)(128)(4,1)} %bitcast.288), calls=%async_computation.5 | async-start | bytes 5767168
  121.4 1.0 copy-start.3
  121.4 1.0 copy-start.5
Sparse Core Ops, SparseCore 0:
  8.9 23.3 all-gather.2
  68.4 21.0 all-gather.4
where the time goes:
time: 132 us; the launch traced here: 131 us
  waiting for transfers between devices  61.2 us (46%)
  matrix products  30 us (23%)
  local copies, waits for them, and re-layouts  14.7 us (11%)
  between operations  14.1 us (11%)
  starting transfers between devices  11.4 us (9%)
    all_gather x2, waiting for transfers between devices, conv_block(): whole = lax.all_gather(local_field, 'chan', axis=1, tiled=True)  44.8 us
    dot_general x54, matrix products, apply_taps(): jnp.einsum('oi,zip->zop', taps_in[first, second, third], window, preferre...  30 us
    ppermute x2, waiting for transfers between devices, with_halo(): before = lax.ppermute(last, axis, up)  16.3 us
    ppermute x2, starting transfers between devices, with_halo(): before = lax.ppermute(last, axis, up)  7.33 us
    unnamed x25, local copies, waits for them, and re-layouts  6.17 us
    slice x10, local copies, waits for them, and re-layouts, apply_taps(): moved = jnp.roll(slab_in, -offset, axis=2) if offset != 0 else slab_in  4.78 us
    ppermute x2, starting transfers between devices, with_halo(): after = lax.ppermute(leading, axis, down)  4.02 us
    slice x2, local copies, waits for them, and re-layouts, with_halo(): leading = lax.slice_in_dim(value, 0, width, axis=dim)  2.71 us
  transfers between devices with their start and end apart: 6, of which 4 were waited for; matrix products, arithmetic and copies ran while one was open for 2% of the time, Pallas kernels for 0%

commit v1 on v0

v1 whole, which is shorter than its diff:
```python
import functools

import jax
import jax.numpy as jnp
from jax import lax
from jax.experimental import pallas as pl
from jax.experimental.pallas import tpu as pltpu
from jax.sharding import PartitionSpec as P

DILATION = 4
NX = 16
HALF = 64
LANES = 128
GROUPS = 2
MESH = pl.DeviceIdType.MESH


def kernel(
    ns, nc, field_ref, w1_hbm, b1_ref, w2_hbm, b2_ref, out_ref,
    planes, w1, w2, part, fin, w_sem, chan_send, chan_recv, halo_send, halo_recv,
):
    s = lax.axis_index("space")
    c = lax.axis_index("chan")
    local = field_ref.shape[1]
    full = local * nc
    has_prev = s > 0
    has_next = s < ns - 1
    prev = jnp.maximum(s - 1, 0)
    following = jnp.minimum(s + 1, ns - 1)

    def rows(owner):
        return pl.ds(pl.multiple_of(owner * local, local), local)

    weight_copies = [
        pltpu.make_async_copy(w1_hbm, w1, w_sem.at[0]),
        pltpu.make_async_copy(w2_hbm, w2, w_sem.at[1]),
    ]
    for copy in weight_copies:
        copy.start()

    barrier = pltpu.get_barrier_semaphore()
    for k in range(1, nc):
        pl.semaphore_signal(barrier, inc=1, device_id=(s, lax.rem(c + k, nc)), device_id_type=MESH)

    @pl.when(has_prev)
    def _():
        pl.semaphore_signal(barrier, inc=1, device_id=(prev, c), device_id_type=MESH)

    @pl.when(has_next)
    def _():
        pl.semaphore_signal(barrier, inc=1, device_id=(following, c), device_id_type=MESH)

    lane = lax.broadcasted_iota(jnp.int32, (local, LANES), 1)
    left = lane < HALF
    for g in range(GROUPS):
        for side in range(2):
            first = field_ref[4 * side + 2 * g].astype(jnp.float32)
            second = field_ref[4 * side + 2 * g + 1].astype(jnp.float32)
            low = jnp.where(left, first, pltpu.roll(second, HALF, 1))
            high = jnp.where(left, pltpu.roll(first, HALF, 1), second)
            planes[0, g, 1 + side, 0, rows(c), :] = low.astype(jnp.bfloat16)
            planes[0, g, 1 + side, 1, rows(c), :] = high.astype(jnp.bfloat16)

    @pl.when(jnp.logical_not(has_prev))
    def _():
        for conv in range(2):
            for g in range(GROUPS):
                planes[conv, g, 0] = jnp.zeros((2, full, LANES), jnp.bfloat16)

    @pl.when(jnp.logical_not(has_next))
    def _():
        for conv in range(2):
            for g in range(GROUPS):
                planes[conv, g, 3] = jnp.zeros((2, full, LANES), jnp.bfloat16)

    pl.semaphore_wait(barrier, nc - 1 + has_prev.astype(jnp.int32) + has_next.astype(jnp.int32))

    def chan_copy(conv, g, side, k):
        where = planes.at[conv, g, 1 + side, :, rows(c), :]
        return pltpu.make_async_remote_copy(
            src_ref=where, dst_ref=where,
            send_sem=chan_send.at[conv, g, side, k], recv_sem=chan_recv.at[conv, g, side, k],
            device_id=(s, lax.rem(c + k, nc)), device_id_type=MESH,
        )

    def chan_arrival(conv, g, side, k):
        owner = lax.rem(c - k + nc, nc)
        where = planes.at[conv, g, 1 + side, :, rows(owner), :]
        return pltpu.make_async_remote_copy(
            src_ref=where, dst_ref=where,
            send_sem=chan_send.at[conv, g, side, k], recv_sem=chan_recv.at[conv, g, side, k],
            device_id=(s, lax.rem(c + k, nc)), device_id_type=MESH,
        )

    def halo_copy(conv, g, side, k):
        owner = lax.rem(c - k + nc, nc)
        return pltpu.make_async_remote_copy(
            src_ref=planes.at[conv, g, 1 + side, :, rows(owner), :],
            dst_ref=planes.at[conv, g, 0 if side == 1 else 3, :, rows(owner), :],
            send_sem=halo_send.at[conv, g, side, k], recv_sem=halo_recv.at[conv, g, side, k],
            device_id=(following if side == 1 else prev, c), device_id_type=MESH,
        )

    def send_halo(conv, g, side, k):
        @pl.when(has_next if side == 1 else has_prev)
        def _():
            halo_copy(conv, g, side, k).start()

    def send_own(conv, g):
        for side in range(2):
            for k in range(1, nc):
                chan_copy(conv, g, side, k).start()
        for side in range(2):
            send_halo(conv, g, side, 0)

    def pass_on(conv, g):
        for side in range(2):
            for k in range(1, nc):
                chan_arrival(conv, g, side, k).wait_recv()
                send_halo(conv, g, side, k)

    def wait_halos(conv, g):
        for side in range(2):
            @pl.when(has_prev if side == 1 else has_next)
            def _():
                for k in range(nc):
                    halo_copy(conv, g, side, k).wait_recv()

    def wait_sends(conv, g):
        for side in range(2):
            for k in range(1, nc):
                chan_copy(conv, g, side, k).wait_send()

            @pl.when(has_next if side == 1 else has_prev)
            def _():
                for k in range(nc):
                    halo_copy(conv, g, side, k).wait_send()

    lane_x = lax.rem(lane, NX)
    from_left = lane_x >= DILATION
    from_right = lane_x < NX - DILATION

    def convolve(conv, g, taps, bias, store):
        for half in range(2):
            for dx in range(3):
                total = None
                for dz in range(3):
                    for other in range(2):
                        window = jnp.concatenate(
                            [planes[conv, g, dz, other], planes[conv, g, dz + 1, other]], axis=1
                        )
                        term = jnp.dot(
                            taps[dz, other - half + 1, dx], window, preferred_element_type=jnp.float32
                        )
                        total = term if total is None else total + term
                part[dx] = total
            for side in range(2):
                cols = pl.ds(side * LANES, LANES)
                pre = part[1, :, cols] + bias
                pre += jnp.where(from_left, pltpu.roll(part[0, :, cols], DILATION, 1), 0.0)
                pre += jnp.where(from_right, pltpu.roll(part[2, :, cols], LANES - DILATION, 1), 0.0)
                value = planes[conv, g, 1 + side, half, rows(c), :].astype(jnp.float32)
                value += jax.nn.gelu(pre, approximate=True)
                store(g, side, half, value)

    def keep(g, side, half, value):
        planes[1, g, 1 + side, half, rows(c), :] = value.astype(jnp.bfloat16)

    def finish(g, side, half, value):
        if half == 0:
            fin[side] = value
        else:
            low = fin[side]
            first = jnp.where(left, low, pltpu.roll(value, HALF, 1))
            second = jnp.where(left, pltpu.roll(low, HALF, 1), value)
            out_ref[4 * side + 2 * g] = first.astype(jnp.bfloat16)
            out_ref[4 * side + 2 * g + 1] = second.astype(jnp.bfloat16)

    for g in range(GROUPS):
        send_own(0, g)
    for conv, (taps, b_ref) in enumerate(((w1, b1_ref), (w2, b2_ref))):
        bias = jnp.transpose(jnp.broadcast_to(b_ref[...], (LANES, local)))
        weight_copies[conv].wait()
        for g in range(GROUPS):
            pass_on(conv, g)
            wait_halos(conv, g)
            convolve(conv, g, taps, bias, keep if conv == 0 else finish)
            if conv == 0:
                send_own(1, g)
    for conv in range(2):
        for g in range(GROUPS):
            wait_sends(conv, g)


def per_device(ns, nc, field_in, kernel_first, bias_first, kernel_second, bias_second):
    layers, local, voxels = field_in.shape
    full = local * nc
    vmem = pl.BlockSpec(memory_space=pltpu.VMEM)
    hbm = pl.BlockSpec(memory_space=pl.ANY)
    dma = pltpu.SemaphoreType.DMA
    return pl.pallas_call(
        functools.partial(kernel, ns, nc),
        out_shape=jax.ShapeDtypeStruct(field_in.shape, jnp.bfloat16),
        in_specs=[vmem, hbm, vmem, hbm, vmem],
        out_specs=vmem,
        scratch_shapes=[
            pltpu.VMEM((2, GROUPS, 4, 2, full, LANES), jnp.bfloat16),
            pltpu.VMEM(kernel_first.shape, jnp.bfloat16),
            pltpu.VMEM(kernel_second.shape, jnp.bfloat16),
            pltpu.VMEM((3, local, 2 * LANES), jnp.float32),
            pltpu.VMEM((2, local, LANES), jnp.float32),
            dma((2,)),
            dma((2, GROUPS, 2, nc)),
            dma((2, GROUPS, 2, nc)),
            dma((2, GROUPS, 2, nc)),
            dma((2, GROUPS, 2, nc)),
        ],
        cost_estimate=pl.CostEstimate(
            flops=2 * 2 * 27 * local * full * layers * voxels,
            bytes_accessed=2 * 27 * local * full * 2,
            transcendentals=2 * layers * local * voxels,
        ),
        compiler_params=pltpu.CompilerParams(
            collective_id=0, has_side_effects=True, vmem_limit_bytes=48 * 1024 * 1024
        ),
    )(field_in, kernel_first, bias_first.reshape(1, local), kernel_second, bias_second.reshape(1, local))


def solution(mesh):
    placed = (
        P("space", "chan", None),
        P(None, None, None, "chan", None),
        P("chan"),
        P(None, None, None, "chan", None),
        P("chan"),
    )
    body = functools.partial(per_device, mesh.shape["space"], mesh.shape["chan"])
    return jax.shard_map(
        body, mesh=mesh, in_specs=placed, out_specs=P("space", "chan", None), check_vma=False
    )
```

time: 132 us -> 45.1 us (0.34)
  waiting for transfers between devices: 61.2 us -> 0 us
  Pallas kernels: 0 us -> 41.7 us
  matrix products: 30 us -> 0 us
  between operations: 14.1 us -> 0.01 us
  local copies, waits for them, and re-layouts: 14.7 us -> 3.19 us
  starting transfers between devices: 11.4 us -> 0 us
    all_gather x2 -> x0, waiting for transfers between devices: 44.8 us -> none  [conv_block(): whole = lax.all_gather(local_field, 'chan', axis=1, tiled=True)]
    pallas_call x0 -> x1, Pallas kernels: none -> 41.7 us  [per_device(): pl.pallas_call(functools.partial(kernel, ns, nc), out_shape=jax.ShapeDtyp...]
    dot_general x54 -> x0, matrix products: 30 us -> none  [apply_taps(): jnp.einsum('oi,zip->zop', taps_in[first, second, third], window, preferre...]
    ppermute x4 -> x0, waiting for transfers between devices: 16.3 us -> none  [the longest x2 16.3 us: with_halo(): before = lax.ppermute(last, axis, up)]
    ppermute x4 -> x0, starting transfers between devices: 11.3 us -> none  [the longest x2 7.33 us: with_halo(): before = lax.ppermute(last, axis, up)]
    slice x12 -> x0, local copies, waits for them, and re-layouts: 7.49 us -> none  [the longest x10 4.78 us: apply_taps(): moved = jnp.roll(slab_in, -offset, axis=2) if offset != 0 else slab_in]
    unnamed x25 -> x7, local copies, waits for them, and re-layouts: 6.17 us -> 3.19 us
  transfers between devices with their start and end apart: 6 -> 0, of which waited for: 4 -> 0; matrix products, arithmetic and copies ran while one was open for 2% -> 0% of each run, Pallas kernels for 0% -> 0%
where the time goes in v1:
time: 45.1 us; the launch traced here: 44.9 us
  Pallas kernels  41.7 us (92%)
  local copies, waits for them, and re-layouts  3.19 us (7%)
    pallas_call x1, Pallas kernels, per_device(): pl.pallas_call(functools.partial(kernel, ns, nc), out_shape=jax.ShapeDtyp...  41.7 us
    unnamed x7, local copies, waits for them, and re-layouts  3.19 us

profile of v1, /device:TPU:1, one launch (start us, length us, event | category | flops | bytes accessed | tf_op | source)
XLA Modules:
  0.0 44.9 jit_solution(11209652271586628143)
XLA Ops:
  0.0 0.0 copy-start
  0.0 1.0 %copy-done = bf16[8,256,128]{2,1,0:T(8,128)(2,1)S(1)} copy-done((bf16[8,256,128]{2,1,0:T(8,128)(2,1)S(1)}, bf16[8,256,128]{2,1,0:T(8,128)(2,1)}, u32[]{:S(2)}) %copy-start) | copy-done | bytes 524312
  1.0 0.0 copy-start.1
  1.0 0.7 %copy-done.1 = f32[256]{0:T(256)S(1)} copy-done((f32[256]{0:T(256)S(1)}, f32[256]{0:T(256)}, u32[]{:S(2)}) %copy-start.1) | copy-done | bytes 1048
  1.7 0.0 copy-start.2
  1.7 0.7 %copy-done.2 = f32[256]{0:T(256)S(1)} copy-done((f32[256]{0:T(256)S(1)}, f32[256]{0:T(256)}, u32[]{:S(2)}) %copy-start.2) | copy-done | bytes 1048
  2.4 41.7 %shard_map.55 = bf16[8,256,128]{2,1,0:T(8,128)(2,1)S(1)} custom-call(bf16[8,256,128]{2,1,0:T(8,128)(2,1)S(1)} %copy-done, bf16[3,3,3,256,512]{4,3,2,1,0:T(8,128)(2,1)} %w1_hbm.1, f32[1,256]{1,0:T(1,128)S(1)} %bitcast.2, bf16[3,3,3,256,512]{4,3,2,1,0:T(8,128)(2,1)} %w2_hbm.1, f32[1,256]{1,0:T(1,128)S(1)} %bitcast.3), custom_call_target="tpu_custom_call" | custom-call | flops 14495514624 | bytes 14155776 | tf_op jit(solution)/shard_map/pallas_call | solution.py:201
  44.1 0.8 %copy.7 = bf16[8,256,128]{2,1,0:T(8,128)(2,1)} copy(bf16[8,256,128]{2,1,0:T(8,128)(2,1)S(1)} %shard_map.55) | data formatting | bytes 1048576
Async XLA Ops:
  0.0 1.0 %copy-start = (bf16[8,256,128]{2,1,0:T(8,128)(2,1)S(1)}, bf16[8,256,128]{2,1,0:T(8,128)(2,1)}, u32[]{:S(2)}) copy-start(bf16[8,256,128]{2,1,0:T(8,128)(2,1)} %field_ref.1) | copy-start | bytes 1572868
  1.0 0.7 %copy-start.1 = (f32[256]{0:T(256)S(1)}, f32[256]{0:T(256)}, u32[]{:S(2)}) copy-start(f32[256]{0:T(256)} %param.7) | copy-start | bytes 3076
  1.7 0.7 %copy-start.2 = (f32[256]{0:T(256)S(1)}, f32[256]{0:T(256)}, u32[]{:S(2)}) copy-start(f32[256]{0:T(256)} %param.9) | copy-start | bytes 3076

commit v2 on v0

v2 whole, which is shorter than its diff:
```python
import functools

import jax
import jax.numpy as jnp
from jax import lax
from jax.experimental import pallas as pl
from jax.experimental.pallas import tpu as pltpu
from jax.sharding import PartitionSpec as P

DILATION = 4
NX = 16
HALF = 64
LANES = 128
GROUPS = 2
MESH = pl.DeviceIdType.MESH


def kernel(
    ns, nc, field_hbm, w1_hbm, b1_hbm, w2_hbm, b2_hbm, out_ref,
    planes, w1, w2, part, field, b1, b2, border_out, border_in, fin,
    load_sem, chan_send, chan_recv, halo_send, halo_recv,
):
    s = lax.axis_index("space")
    c = lax.axis_index("chan")
    local = field.shape[1]
    has_prev = s > 0
    has_next = s < ns - 1
    prev = jnp.maximum(s - 1, 0)
    following = jnp.minimum(s + 1, ns - 1)
    split = local % LANES == 0

    def rows(owner):
        return pl.ds(pl.multiple_of(owner * local, local), local)

    barrier = pltpu.get_barrier_semaphore()
    for k in range(1, nc):
        pl.semaphore_signal(barrier, inc=1, device_id=(s, lax.rem(c + k, nc)), device_id_type=MESH)

    @pl.when(has_prev)
    def _():
        pl.semaphore_signal(barrier, inc=1, device_id=(prev, c), device_id_type=MESH)

    @pl.when(has_next)
    def _():
        pl.semaphore_signal(barrier, inc=1, device_id=(following, c), device_id_type=MESH)

    loads = [
        pltpu.make_async_copy(source, target, load_sem.at[n])
        for n, (source, target) in enumerate(
            ((field_hbm, field), (b1_hbm, b1), (b2_hbm, b2), (w1_hbm, w1), (w2_hbm, w2))
        )
    ]
    for load in loads:
        load.start()

    lane = lax.broadcasted_iota(jnp.int32, (local, LANES), 1)
    left = lane < HALF
    lane_x = lax.rem(lane, NX)
    from_left = lane_x >= DILATION
    from_right = lane_x < NX - DILATION

    def chan_copy(conv, g, k, owner):
        where = planes.at[conv, g, :, :, rows(owner), :]
        return pltpu.make_async_remote_copy(
            src_ref=where, dst_ref=where,
            send_sem=chan_send.at[conv, g, k], recv_sem=chan_recv.at[conv, g, k],
            device_id=(s, lax.rem(c + k, nc)), device_id_type=MESH,
        )

    def halo_copy(conv, g, up):
        return pltpu.make_async_remote_copy(
            src_ref=border_out.at[conv, g, up], dst_ref=border_in.at[conv, g, 1 - up],
            send_sem=halo_send.at[conv, g, up], recv_sem=halo_recv.at[conv, g, up],
            device_id=(following if up == 1 else prev, c), device_id_type=MESH,
        )

    def send_own(conv, g):
        for k in range(1, nc):
            chan_copy(conv, g, k, c).start()

    def wait_chan(conv, g):
        for k in range(1, nc):
            chan_copy(conv, g, k, lax.rem(c - k + nc, nc)).wait_recv()

    def send_halo(conv, g):
        for up in range(2):
            @pl.when(has_next if up == 1 else has_prev)
            def _():
                halo_copy(conv, g, up).start()

    def wait_halo(conv, g):
        for up in range(2):
            @pl.when(has_prev if up == 1 else has_next)
            def _():
                halo_copy(conv, g, up).wait_recv()

    def wait_sends(conv, g):
        for k in range(1, nc):
            chan_copy(conv, g, k, c).wait_send()
        for up in range(2):
            @pl.when(has_next if up == 1 else has_prev)
            def _():
                halo_copy(conv, g, up).wait_send()

    def multiply(conv, g, dz, taps, block, first):
        for half in range(2):
            total = None
            for other in range(2):
                window = jnp.concatenate(
                    [planes[conv, g, 0, other, block, :], planes[conv, g, 1, other, block, :]], axis=1
                )
                stack = taps[dz, other - half + 1, :, :, block]
                term = jnp.dot(
                    stack.reshape(3 * local, window.shape[0]), window, preferred_element_type=jnp.float32
                )
                total = term if total is None else total + term
            total = total.reshape(3, local, 2 * LANES)
            if first:
                part[g, dz, half] = total
            else:
                part[g, dz, half] += total

    def shifted(pick):
        value = pick(1)
        value += jnp.where(from_left, pltpu.roll(pick(0), DILATION, 1), 0.0)
        return value + jnp.where(from_right, pltpu.roll(pick(2), LANES - DILATION, 1), 0.0)

    lo, hi = pl.ds(0, LANES), pl.ds(LANES, LANES)

    def multiply_own(conv, g, taps):
        if split:
            for dz in (0, 2, 1):
                multiply(conv, g, dz, taps, rows(c), True)

    def multiply_rest(conv, g, taps):
        if split:
            blocks = [rows(lax.rem(c - k + nc, nc)) for k in range(1, nc)]
        else:
            blocks = [pl.ds(0, local * nc)]
        for dz in (0, 2, 1):
            for n, block in enumerate(blocks):
                multiply(conv, g, dz, taps, block, n == 0 and not split)
            if dz == 1:
                continue
            up, cols = (1, hi) if dz == 0 else (0, lo)
            for half in range(2):
                value = shifted(lambda dx: part[g, dz, half, dx, :, cols])
                border_out[conv, g, up, half] = value.astype(jnp.bfloat16)

            @pl.when(has_next if up == 1 else has_prev)
            def _():
                halo_copy(conv, g, up).start()

    def conclude(conv, g, bias, store):
        for side in range(2):
            dz, mine, cross = (2, lo, hi) if side == 0 else (0, hi, lo)
            for half in range(2):
                pre = shifted(lambda dx: part[g, 1, half, dx, :, mine] + part[g, dz, half, dx, :, cross])
                pre += border_in[conv, g, side, half].astype(jnp.float32) + bias
                value = planes[conv, g, side, half, rows(c), :].astype(jnp.float32)
                value += jax.nn.gelu(pre, approximate=True)
                store(g, side, half, value)

    def keep(g, side, half, value):
        planes[1, g, side, half, rows(c), :] = value.astype(jnp.bfloat16)

    def finish(g, side, half, value):
        if half == 0:
            fin[...] = value
        else:
            low = fin[...]
            first = jnp.where(left, low, pltpu.roll(value, HALF, 1))
            second = jnp.where(left, pltpu.roll(low, HALF, 1), value)
            out_ref[4 * side + 2 * g] = first.astype(jnp.bfloat16)
            out_ref[4 * side + 2 * g + 1] = second.astype(jnp.bfloat16)

    def pack(g):
        for side in range(2):
            first = field[4 * side + 2 * g].astype(jnp.float32)
            second = field[4 * side + 2 * g + 1].astype(jnp.float32)
            low = jnp.where(left, first, pltpu.roll(second, HALF, 1))
            high = jnp.where(left, pltpu.roll(first, HALF, 1), second)
            planes[0, g, side, 0, rows(c), :] = low.astype(jnp.bfloat16)
            planes[0, g, side, 1, rows(c), :] = high.astype(jnp.bfloat16)

    loads[0].wait()
    pack(0)
    pl.semaphore_wait(barrier, nc - 1 + has_prev.astype(jnp.int32) + has_next.astype(jnp.int32))
    send_own(0, 0)
    pack(1)
    send_own(0, 1)

    @pl.when(jnp.logical_not(has_prev))
    def _():
        for conv in range(2):
            for g in range(GROUPS):
                border_in[conv, g, 0] = jnp.zeros((2, local, LANES), jnp.bfloat16)

    @pl.when(jnp.logical_not(has_next))
    def _():
        for conv in range(2):
            for g in range(GROUPS):
                border_in[conv, g, 1] = jnp.zeros((2, local, LANES), jnp.bfloat16)

    loads[1].wait()
    loads[2].wait()
    bias1 = jnp.transpose(jnp.broadcast_to(b1[...], (LANES, local)))
    bias2 = jnp.transpose(jnp.broadcast_to(b2[...], (LANES, local)))
    loads[3].wait()
    multiply_own(0, 0, w1)
    multiply_own(0, 1, w1)
    wait_chan(0, 0)
    multiply_rest(0, 0, w1)
    loads[4].wait()
    wait_halo(0, 0)
    conclude(0, 0, bias1, keep)
    send_own(1, 0)
    wait_chan(0, 1)
    multiply_rest(0, 1, w1)
    multiply_own(1, 0, w2)
    wait_halo(0, 1)
    conclude(0, 1, bias1, keep)
    send_own(1, 1)
    multiply_own(1, 1, w2)
    for g in range(GROUPS):
        wait_chan(1, g)
        multiply_rest(1, g, w2)
        wait_halo(1, g)
        conclude(1, g, bias2, finish)
    for conv in range(2):
        for g in range(GROUPS):
            wait_sends(conv, g)


def per_device(ns, nc, field_in, kernel_first, bias_first, kernel_second, bias_second):
    layers, local, voxels = field_in.shape
    full = local * nc
    hbm = pl.BlockSpec(memory_space=pltpu.HBM)
    dma = pltpu.SemaphoreType.DMA
    border = pltpu.VMEM((2, GROUPS, 2, 2, local, LANES), jnp.bfloat16)
    return pl.pallas_call(
        functools.partial(kernel, ns, nc),
        out_shape=jax.ShapeDtypeStruct(field_in.shape, jnp.bfloat16),
        in_specs=[hbm] * 5,
        out_specs=pl.BlockSpec(memory_space=pltpu.VMEM),
        scratch_shapes=[
            pltpu.VMEM((2, GROUPS, 2, 2, full, LANES), jnp.bfloat16),
            pltpu.VMEM(kernel_first.shape, jnp.bfloat16),
            pltpu.VMEM(kernel_second.shape, jnp.bfloat16),
            pltpu.VMEM((GROUPS, 3, 2, 3, local, 2 * LANES), jnp.float32),
            pltpu.VMEM(field_in.shape, jnp.bfloat16),
            pltpu.VMEM((1, local), jnp.float32),
            pltpu.VMEM((1, local), jnp.float32),
            border,
            border,
            pltpu.VMEM((local, LANES), jnp.float32),
            dma((5,)),
            dma((2, GROUPS, nc)),
            dma((2, GROUPS, nc)),
            dma((2, GROUPS, 2)),
            dma((2, GROUPS, 2)),
        ],
        cost_estimate=pl.CostEstimate(
            flops=2 * 2 * 27 * local * full * layers * voxels,
            bytes_accessed=2 * 27 * local * full * 2,
            transcendentals=2 * layers * local * voxels,
        ),
        compiler_params=pltpu.CompilerParams(
            collective_id=0, has_side_effects=True, vmem_limit_bytes=50 * 1024 * 1024
        ),
    )(field_in, kernel_first, bias_first.reshape(1, local), kernel_second, bias_second.reshape(1, local))


def solution(mesh):
    placed = (
        P("space", "chan", None),
        P(None, None, None, "chan", None),
        P("chan"),
        P(None, None, None, "chan", None),
        P("chan"),
    )
    body = functools.partial(per_device, mesh.shape["space"], mesh.shape["chan"])
    return jax.shard_map(
        body, mesh=mesh, in_specs=placed, out_specs=P("space", "chan", None), check_vma=False
    )
```

time: 132 us -> 39.3 us (0.30)
  waiting for transfers between devices: 61.2 us -> 0 us
  Pallas kernels: 0 us -> 35.9 us
  matrix products: 30 us -> 0 us
  between operations: 14.1 us -> 0.01 us
  local copies, waits for them, and re-layouts: 14.7 us -> 3.19 us
  starting transfers between devices: 11.4 us -> 0 us
    all_gather x2 -> x0, waiting for transfers between devices: 44.8 us -> none  [conv_block(): whole = lax.all_gather(local_field, 'chan', axis=1, tiled=True)]
    pallas_call x0 -> x1, Pallas kernels: none -> 35.9 us  [per_device(): pl.pallas_call(functools.partial(kernel, ns, nc), out_shape=jax.ShapeDtyp...]
    dot_general x54 -> x0, matrix products: 30 us -> none  [apply_taps(): jnp.einsum('oi,zip->zop', taps_in[first, second, third], window, preferre...]
    ppermute x4 -> x0, waiting for transfers between devices: 16.3 us -> none  [the longest x2 16.3 us: with_halo(): before = lax.ppermute(last, axis, up)]
    ppermute x4 -> x0, starting transfers between devices: 11.3 us -> none  [the longest x2 7.33 us: with_halo(): before = lax.ppermute(last, axis, up)]
    slice x12 -> x0, local copies, waits for them, and re-layouts: 7.49 us -> none  [the longest x10 4.78 us: apply_taps(): moved = jnp.roll(slab_in, -offset, axis=2) if offset != 0 else slab_in]
    unnamed x25 -> x7, local copies, waits for them, and re-layouts: 6.17 us -> 3.19 us
  transfers between devices with their start and end apart: 6 -> 0, of which waited for: 4 -> 0; matrix products, arithmetic and copies ran while one was open for 2% -> 0% of each run, Pallas kernels for 0% -> 0%
where the time goes in v2:
time: 39.3 us; the launch traced here: 39.1 us
  Pallas kernels  35.9 us (91%)
  local copies, waits for them, and re-layouts  3.19 us (8%)
    pallas_call x1, Pallas kernels, per_device(): pl.pallas_call(functools.partial(kernel, ns, nc), out_shape=jax.ShapeDtyp...  35.9 us
    unnamed x7, local copies, waits for them, and re-layouts  3.19 us

profile of v2, /device:TPU:1, one launch (start us, length us, event | category | flops | bytes accessed | tf_op | source)
XLA Modules:
  0.0 39.1 jit_solution(17925683645300225638)
XLA Ops:
  0.0 0.0 copy-start
  0.0 1.0 %copy-done = bf16[8,256,128]{2,1,0:T(8,128)(2,1)S(1)} copy-done((bf16[8,256,128]{2,1,0:T(8,128)(2,1)S(1)}, bf16[8,256,128]{2,1,0:T(8,128)(2,1)}, u32[]{:S(2)}) %copy-start) | copy-done | bytes 524312
  1.0 0.0 copy-start.1
  1.0 0.7 %copy-done.1 = f32[256]{0:T(256)S(1)} copy-done((f32[256]{0:T(256)S(1)}, f32[256]{0:T(256)}, u32[]{:S(2)}) %copy-start.1) | copy-done | bytes 1048
  1.7 0.0 copy-start.2
  1.7 0.7 %copy-done.2 = f32[256]{0:T(256)S(1)} copy-done((f32[256]{0:T(256)S(1)}, f32[256]{0:T(256)}, u32[]{:S(2)}) %copy-start.2) | copy-done | bytes 1048
  2.4 35.9 %shard_map.55 = bf16[8,256,128]{2,1,0:T(8,128)(2,1)S(1)} custom-call(bf16[8,256,128]{2,1,0:T(8,128)(2,1)S(1)} %copy-done, bf16[3,3,3,256,512]{4,3,2,1,0:T(8,128)(2,1)} %w1_hbm.1, f32[1,256]{1,0:T(1,128)S(1)} %bitcast.2, bf16[3,3,3,256,512]{4,3,2,1,0:T(8,128)(2,1)} %w2_hbm.1, f32[1,256]{1,0:T(1,128)S(1)} %bitcast.3), custom_call_target="tpu_custom_call" | custom-call | flops 14495514624 | bytes 14155776 | tf_op jit(solution)/shard_map/pallas_call | solution.py:241
  38.3 0.8 %copy.7 = bf16[8,256,128]{2,1,0:T(8,128)(2,1)} copy(bf16[8,256,128]{2,1,0:T(8,128)(2,1)S(1)} %shard_map.55) | data formatting | bytes 1048576
Async XLA Ops:
  0.0 1.0 %copy-start = (bf16[8,256,128]{2,1,0:T(8,128)(2,1)S(1)}, bf16[8,256,128]{2,1,0:T(8,128)(2,1)}, u32[]{:S(2)}) copy-start(bf16[8,256,128]{2,1,0:T(8,128)(2,1)} %field_hbm.1) | copy-start | bytes 1572868
  1.0 0.7 %copy-start.1 = (f32[256]{0:T(256)S(1)}, f32[256]{0:T(256)}, u32[]{:S(2)}) copy-start(f32[256]{0:T(256)} %param.7) | copy-start | bytes 3076
  1.7 0.7 %copy-start.2 = (f32[256]{0:T(256)S(1)}, f32[256]{0:T(256)}, u32[]{:S(2)}) copy-start(f32[256]{0:T(256)} %param.9) | copy-start | bytes 3076

commit v3 on v2

v3 whole, which is shorter than its diff:
```python
import functools

import jax
import jax.numpy as jnp
from jax import lax
from jax.experimental import pallas as pl
from jax.experimental.pallas import tpu as pltpu
from jax.sharding import PartitionSpec as P

DILATION = 4
NX = 16
HALF = 64
LANES = 128
GROUPS = 4
MESH = pl.DeviceIdType.MESH


def kernel(
    ns, nc, field_hbm, w1_hbm, b1_hbm, w2_hbm, b2_hbm, out_ref,
    planes, w1, w2, part, field, b1, b2, border_out, border_in,
    load_sem, chan_send, chan_recv, halo_send, halo_recv,
):
    s = lax.axis_index("space")
    c = lax.axis_index("chan")
    local = field.shape[1]
    has_prev = s > 0
    has_next = s < ns - 1
    prev = jnp.maximum(s - 1, 0)
    following = jnp.minimum(s + 1, ns - 1)
    split = local % LANES == 0

    def rows(owner):
        return pl.ds(pl.multiple_of(owner * local, local), local)

    barrier = pltpu.get_barrier_semaphore()
    for k in range(1, nc):
        pl.semaphore_signal(barrier, inc=1, device_id=(s, lax.rem(c + k, nc)), device_id_type=MESH)

    @pl.when(has_prev)
    def _():
        pl.semaphore_signal(barrier, inc=1, device_id=(prev, c), device_id_type=MESH)

    @pl.when(has_next)
    def _():
        pl.semaphore_signal(barrier, inc=1, device_id=(following, c), device_id_type=MESH)

    loads = [
        pltpu.make_async_copy(source, target, load_sem.at[n])
        for n, (source, target) in enumerate(
            ((field_hbm, field), (b1_hbm, b1), (b2_hbm, b2), (w1_hbm, w1), (w2_hbm, w2))
        )
    ]
    for load in loads:
        load.start()

    lane = lax.broadcasted_iota(jnp.int32, (local, LANES), 1)
    left = lane < HALF
    lane_x = lax.rem(lane, NX)
    from_left = lane_x >= DILATION
    from_right = lane_x < NX - DILATION

    def chan_copy(conv, g, k, owner):
        where = planes.at[conv, g, :, rows(owner), :]
        return pltpu.make_async_remote_copy(
            src_ref=where, dst_ref=where,
            send_sem=chan_send.at[conv, g, k], recv_sem=chan_recv.at[conv, g, k],
            device_id=(s, lax.rem(c + k, nc)), device_id_type=MESH,
        )

    def halo_copy(conv, g, up):
        return pltpu.make_async_remote_copy(
            src_ref=border_out.at[conv, g, up], dst_ref=border_in.at[conv, g, 1 - up],
            send_sem=halo_send.at[conv, g, up], recv_sem=halo_recv.at[conv, g, up],
            device_id=(following if up == 1 else prev, c), device_id_type=MESH,
        )

    def send_own(conv, g):
        for k in range(1, nc):
            chan_copy(conv, g, k, c).start()

    def wait_chan(conv, g):
        for k in range(1, nc):
            chan_copy(conv, g, k, lax.rem(c - k + nc, nc)).wait_recv()

    def wait_halo(conv, g):
        for up in range(2):
            @pl.when(has_prev if up == 1 else has_next)
            def _():
                halo_copy(conv, g, up).wait_recv()

    def wait_sends(conv, g):
        for k in range(1, nc):
            chan_copy(conv, g, k, c).wait_send()
        for up in range(2):
            @pl.when(has_next if up == 1 else has_prev)
            def _():
                halo_copy(conv, g, up).wait_send()

    def multiply(conv, g, dz, taps, block, first):
        low, high = planes[conv, g, 0, block, :], planes[conv, g, 1, block, :]

        def product(dy, window):
            stack = taps[dz, dy, :, :, block].reshape(3 * local, window.shape[0])
            return jnp.dot(stack, window, preferred_element_type=jnp.float32)

        both = product(1, jnp.concatenate([low, high], axis=1))
        for half, term in ((0, product(2, high)), (1, product(0, low))):
            total = both[:, half * LANES : (half + 1) * LANES] + term
            total = total.reshape(3, local, LANES)
            if first:
                part[g, dz, half] = total
            else:
                part[g, dz, half] += total

    def swapped(value):
        return pltpu.roll(value, HALF, 1)

    def exchanged(first, second):
        return jnp.where(left, first, swapped(second)), jnp.where(left, swapped(first), second)

    def shifted(pick):
        value = pick(1)
        value += jnp.where(from_left, pltpu.roll(pick(0), DILATION, 1), 0.0)
        return value + jnp.where(from_right, pltpu.roll(pick(2), LANES - DILATION, 1), 0.0)

    def multiply_own(conv, g, taps):
        if split:
            for dz in (0, 2, 1):
                multiply(conv, g, dz, taps, rows(c), True)

    def multiply_rest(conv, g, taps):
        if split:
            blocks = [rows(lax.rem(c - k + nc, nc)) for k in range(1, nc)]
        else:
            blocks = [pl.ds(0, local * nc)]
        for dz in (0, 2, 1):
            for n, block in enumerate(blocks):
                multiply(conv, g, dz, taps, block, n == 0 and not split)
            if dz != 2:
                continue
            outer = [
                shifted(lambda dx: jnp.where(left, part[g, 2, half, dx], part[g, 0, half, dx]))
                for half in range(2)
            ]
            for up, value in enumerate(exchanged(*outer)):
                border_out[conv, g, up] = value.astype(jnp.bfloat16)
            for up in range(2):
                @pl.when(has_next if up == 1 else has_prev)
                def _():
                    halo_copy(conv, g, up).start()

    def conclude(conv, g, bias, store):
        wait_halo(conv, g)
        arrived = exchanged(
            border_in[conv, g, 0].astype(jnp.float32), border_in[conv, g, 1].astype(jnp.float32)
        )
        values = []
        for half in range(2):
            pre = shifted(
                lambda dx: part[g, 1, half, dx]
                + swapped(jnp.where(left, part[g, 0, half, dx], part[g, 2, half, dx]))
            )
            pre += arrived[half] + bias
            value = planes[conv, g, half, rows(c), :].astype(jnp.float32)
            values.append(value + jax.nn.gelu(pre, approximate=True))
        store(g, values)

    def keep(g, values):
        for half in range(2):
            planes[1, g, half, rows(c), :] = values[half].astype(jnp.bfloat16)

    def finish(g, values):
        for side, value in enumerate(exchanged(*values)):
            out_ref[4 * side + g] = value.astype(jnp.bfloat16)

    def pack(g):
        layers = exchanged(field[g].astype(jnp.float32), field[4 + g].astype(jnp.float32))
        for half in range(2):
            planes[0, g, half, rows(c), :] = layers[half].astype(jnp.bfloat16)

    loads[0].wait()
    pack(0)
    pl.semaphore_wait(barrier, nc - 1 + has_prev.astype(jnp.int32) + has_next.astype(jnp.int32))
    send_own(0, 0)
    for g in range(1, GROUPS):
        pack(g)
        send_own(0, g)

    @pl.when(jnp.logical_not(has_prev))
    def _():
        for conv in range(2):
            for g in range(GROUPS):
                border_in[conv, g, 0] = jnp.zeros((local, LANES), jnp.bfloat16)

    @pl.when(jnp.logical_not(has_next))
    def _():
        for conv in range(2):
            for g in range(GROUPS):
                border_in[conv, g, 1] = jnp.zeros((local, LANES), jnp.bfloat16)

    loads[1].wait()
    loads[2].wait()
    bias1 = jnp.transpose(jnp.broadcast_to(b1[...], (LANES, local)))
    bias2 = jnp.transpose(jnp.broadcast_to(b2[...], (LANES, local)))
    loads[3].wait()
    for g in range(GROUPS):
        multiply_own(0, g, w1)
    for g in range(GROUPS):
        wait_chan(0, g)
        multiply_rest(0, g, w1)
        if g == 0:
            loads[4].wait()
        else:
            conclude(0, g - 1, bias1, keep)
            send_own(1, g - 1)
        if g > 1:
            multiply_own(1, g - 2, w2)
    multiply_own(1, GROUPS - 2, w2)
    conclude(0, GROUPS - 1, bias1, keep)
    send_own(1, GROUPS - 1)
    multiply_own(1, GROUPS - 1, w2)
    for g in range(GROUPS):
        wait_chan(1, g)
        multiply_rest(1, g, w2)
        if g > 0:
            conclude(1, g - 1, bias2, finish)
    conclude(1, GROUPS - 1, bias2, finish)
    for conv in range(2):
        for g in range(GROUPS):
            wait_sends(conv, g)


def per_device(ns, nc, field_in, kernel_first, bias_first, kernel_second, bias_second):
    layers, local, voxels = field_in.shape
    full = local * nc
    hbm = pl.BlockSpec(memory_space=pltpu.HBM)
    dma = pltpu.SemaphoreType.DMA
    border = pltpu.VMEM((2, GROUPS, 2, local, LANES), jnp.bfloat16)
    return pl.pallas_call(
        functools.partial(kernel, ns, nc),
        out_shape=jax.ShapeDtypeStruct(field_in.shape, jnp.bfloat16),
        in_specs=[hbm] * 5,
        out_specs=pl.BlockSpec(memory_space=pltpu.VMEM),
        scratch_shapes=[
            pltpu.VMEM((2, GROUPS, 2, full, LANES), jnp.bfloat16),
            pltpu.VMEM(kernel_first.shape, jnp.bfloat16),
            pltpu.VMEM(kernel_second.shape, jnp.bfloat16),
            pltpu.VMEM((GROUPS, 3, 2, 3, local, LANES), jnp.float32),
            pltpu.VMEM(field_in.shape, jnp.bfloat16),
            pltpu.VMEM((1, local), jnp.float32),
            pltpu.VMEM((1, local), jnp.float32),
            border,
            border,
            dma((5,)),
            dma((2, GROUPS, nc)),
            dma((2, GROUPS, nc)),
            dma((2, GROUPS, 2)),
            dma((2, GROUPS, 2)),
        ],
        cost_estimate=pl.CostEstimate(
            flops=2 * 2 * 27 * local * full * layers * voxels,
            bytes_accessed=2 * 27 * local * full * 2,
            transcendentals=2 * layers * local * voxels,
        ),
        compiler_params=pltpu.CompilerParams(
            collective_id=0, has_side_effects=True, vmem_limit_bytes=60 * 1024 * 1024
        ),
    )(field_in, kernel_first, bias_first.reshape(1, local), kernel_second, bias_second.reshape(1, local))


def solution(mesh):
    placed = (
        P("space", "chan", None),
        P(None, None, None, "chan", None),
        P("chan"),
        P(None, None, None, "chan", None),
        P("chan"),
    )
    body = functools.partial(per_device, mesh.shape["space"], mesh.shape["chan"])
    return jax.shard_map(
        body, mesh=mesh, in_specs=placed, out_specs=P("space", "chan", None), check_vma=False
    )
```

time: 39.3 us -> 38.3 us (0.975)
  local copies, waits for them, and re-layouts: 3.19 us -> 1.87 us
    unnamed x7 -> x1, local copies, waits for them, and re-layouts: 3.19 us -> 1.87 us
where the time goes in v3:
time: 38.3 us; the launch traced here: 38.1 us
  Pallas kernels  36.2 us (95%)
  local copies, waits for them, and re-layouts  1.87 us (5%)
    pallas_call x1, Pallas kernels, per_device(): pl.pallas_call(functools.partial(kernel, ns, nc), out_shape=jax.ShapeDtyp...  36.2 us
    unnamed x1, local copies, waits for them, and re-layouts  1.87 us

profile of v3, /device:TPU:1, one launch (start us, length us, event | category | flops | bytes accessed | tf_op | source)
XLA Modules:
  0.0 38.1 jit_solution(16863509552261027144)
XLA Ops:
  0.0 36.2 %shard_map.55 = bf16[8,256,128]{2,1,0:T(8,128)(2,1)} custom-call(bf16[8,256,128]{2,1,0:T(8,128)(2,1)} %field_hbm.1, bf16[3,3,3,256,512]{4,3,2,1,0:T(8,128)(2,1)} %w1_hbm.1, f32[1,256]{1,0:T(1,128)} %bitcast.2, bf16[3,3,3,256,512]{4,3,2,1,0:T(8,128)(2,1)} %w2_hbm.1, f32[1,256]{1,0:T(1,128)} %bitcast.3), custom_call_target="tpu_custom_call" | custom-call | flops 14495514624 | bytes 14155776 | tf_op jit(solution)/shard_map/pallas_call | solution.py:239
  36.2 1.9 %copy.7 = bf16[8,256,128]{2,1,0:T(8,128)(2,1)} copy(bf16[8,256,128]{2,1,0:T(8,128)(2,1)} %shard_map.55) | data formatting | bytes 1048576
